TPU v7x, 32 devices: a whole 2x2x4 slice. The times are simulated.
32 devices in a mesh: groups: 2 (over y), dp: 4 (over z), tensor: 2 (over x), pipe: 2 (over core).
Axes of the slice: x: 2, y: 2, z: 4, core: 2. Of those that a mesh axis runs over, the one named last changes fastest.
Arguments:
- acts: bfloat16 [8192, 8192], P(('groups', 'dp'), ('tensor', 'pipe')), parts along dimension 0, may hold values from -6 to 6
- frozen_value_weight: bfloat16 [8192, 1024], P(('tensor', 'pipe'), 'dp'), may hold values from -0.0625 to 0.0625
- adapter_down_maps: bfloat16 [16, 8192, 64], P('dp', ('tensor', 'pipe')), may hold values from -0.0625 to 0.0625
- adapter_up_maps: bfloat16 [16, 64, 1024], P('dp', None, ('tensor', 'pipe')), may hold values from -0.75 to 0.75
- output_gradient: bfloat16 [8192, 1024], P(('groups', 'dp'), ('tensor', 'pipe')), parts along dimension 0, may hold values from -6 to 6
- token_adapter: int32 [8192, 1], P(('groups', 'dp')), parts along dimension 0, may hold values from 0 to 15; in each aligned block of 1024 rows (0 to 1023, 1024 to 2047, ...) at most 96 rows name the same one
- adapter_slot: int32 [16], replicated, may hold values from 0 to 15, each once
Outputs:
- layer_out: bfloat16 [8192, 1024], P(('groups', 'dp'), ('tensor', 'pipe')), parts along dimension 0
- input_gradient: bfloat16 [8192, 8192], P(('groups', 'dp'), ('tensor', 'pipe')), parts along dimension 0
- grad_down: float32 [32, 8192, 64], P(('groups', 'dp'), ('tensor', 'pipe')), parts along dimension 0
- grad_up: float32 [32, 64, 1024], P(('groups', 'dp'), None, ('tensor', 'pipe')), parts along dimension 0
There are 2 independent parts, one for each index of `groups`. A program takes and returns all parts, laid end to end along the dimension named above; an argument that names none is the same for every part. Nothing has to cross between parts.
Inputs may be any that keep to these rules, and one draw needn't show every extreme that they name: `token_adapter`: within the rows of one device (aligned blocks of 1024 rows) no adapter is named by more than 96 rows, a bound that some block reaches; every adapter is named by some row. Each slot once; adapter a's maps lie at slot adapter_slot[a], which index dp number adapter_slot[a] // 4 holds.
All inputs are finite; a program needn't handle non-finite values.
Results may differ from a plain program's by a relative error of at most 0.015.
Values may be sent and summed in bfloat16 or wider, within the bound.
A program may use at most 128 MiB of HBM per device.

v0:
```python
import jax
import jax.numpy as jnp
from jax import lax
from jax.sharding import PartitionSpec as P

adapter_scale = 2.0


def local(
    acts,
    frozen_value_weight,
    adapter_down_maps,
    adapter_up_maps,
    output_gradient,
    token_adapter,
    adapter_slot,
):
    dp_size = lax.axis_size("dp")
    adapters_per_shard = adapter_down_maps.shape[0]
    tok_dev = acts.shape[0]
    adapters = adapter_slot.shape[0]
    share = tok_dev // (adapters_per_shard * dp_size)
    slots_each = max(2, share + share // 2)
    token_ids = token_adapter[:, 0]
    everyone = jnp.arange(adapters, dtype=jnp.int32)
    chosen = (token_ids[:, None] == everyone[None, :]).astype(jnp.int32)
    slot_tok = jnp.sum(chosen * adapter_slot[None, :], axis=1)
    before = jnp.sum((jnp.cumsum(chosen, axis=0) - chosen) * chosen, axis=1)
    position = slot_tok * slots_each + before
    totals = lax.psum(jnp.sum(chosen, axis=0).astype(jnp.float32), "dp")
    own_slots = lax.axis_index("dp") * adapters_per_shard + jnp.arange(
        adapters_per_shard, dtype=jnp.int32
    )
    local_counts = jnp.sum(
        (adapter_slot[None, :] == own_slots[:, None]).astype(jnp.float32) * totals[None, :], axis=1
    )

    def pack_rows(token_rows):
        buffer = jnp.zeros((adapters * slots_each, token_rows.shape[1]), token_rows.dtype)
        buffer = buffer.at[position].set(token_rows)
        return buffer.reshape(dp_size, adapters_per_shard, slots_each, token_rows.shape[1])

    def restore_rows(buffer):
        return buffer.reshape(adapters * slots_each, buffer.shape[3])[position]

    grad_full = lax.all_gather(output_gradient, ("tensor", "pipe"), axis=1, tiled=True)
    base_terms = jnp.dot(
        acts,
        lax.all_gather(frozen_value_weight, "dp", axis=1, tiled=True),
        preferred_element_type=jnp.float32,
    )
    frozen_back_grad = lax.dot_general(
        grad_full,
        lax.all_gather(frozen_value_weight, "dp", axis=1, tiled=True),
        (((1,), (1,)), ((), ())),
        preferred_element_type=jnp.float32,
    )
    base_out = lax.psum_scatter(
        base_terms.astype(jnp.bfloat16), ("tensor", "pipe"), scatter_dimension=1, tiled=True
    ).astype(jnp.float32)
    send_x = pack_rows(acts)
    send_dy = pack_rows(output_gradient)
    received_input = lax.all_to_all(send_x, "dp", split_axis=0, concat_axis=0, tiled=True)
    rank_space_rows = lax.psum(
        jnp.einsum(
            "fuxn,unz->fuxz", received_input, adapter_down_maps, preferred_element_type=jnp.float32
        ).astype(jnp.bfloat16),
        ("tensor", "pipe"),
    )
    delta_back = lax.all_to_all(
        (
            adapter_scale
            * jnp.einsum(
                "ykzl,klb->ykzb",
                rank_space_rows,
                adapter_up_maps,
                preferred_element_type=jnp.float32,
            )
        ).astype(jnp.bfloat16),
        "dp",
        split_axis=0,
        concat_axis=0,
        tiled=True,
    )
    received_output_grad = lax.all_to_all(send_dy, "dp", split_axis=0, concat_axis=0, tiled=True)
    rank_space_gradient = (
        adapter_scale
        * lax.psum(
            jnp.einsum(
                "ewux,wzx->ewuz",
                received_output_grad,
                adapter_up_maps,
                preferred_element_type=jnp.float32,
            ).astype(jnp.bfloat16),
            ("tensor", "pipe"),
        ).astype(jnp.float32)
    ).astype(jnp.bfloat16)
    adapter_back_grad = lax.all_to_all(
        jnp.einsum(
            "atci,tpi->atcp",
            rank_space_gradient,
            adapter_down_maps,
            preferred_element_type=jnp.float32,
        ).astype(jnp.bfloat16),
        "dp",
        split_axis=0,
        concat_axis=0,
        tiled=True,
    )
    grad_down = (
        jnp.einsum(
            "sjmd,sjmr->jdr",
            received_input,
            rank_space_gradient,
            preferred_element_type=jnp.float32,
        )
        * (1.0 / local_counts)[:, None, None]
    )
    grad_up = (
        jnp.einsum(
            "sjmr,sjmc->jrc",
            rank_space_rows,
            received_output_grad,
            preferred_element_type=jnp.float32,
        )
        * (adapter_scale / local_counts)[:, None, None]
    )
    layer_out = (base_out + restore_rows(delta_back).astype(jnp.float32)).astype(jnp.bfloat16)
    input_gradient = (
        frozen_back_grad + restore_rows(adapter_back_grad).astype(jnp.float32)
    ).astype(jnp.bfloat16)
    return (layer_out, input_gradient, grad_down, grad_up)


def solution(mesh):
    return jax.shard_map(
        local,
        mesh=mesh,
        in_specs=(
            P(("groups", "dp"), ("tensor", "pipe")),
            P(("tensor", "pipe"), "dp"),
            P("dp", ("tensor", "pipe"), None),
            P("dp", None, ("tensor", "pipe")),
            P(("groups", "dp"), ("tensor", "pipe")),
            P(("groups", "dp"), None),
            P(),
        ),
        out_specs=(
            P(("groups", "dp"), ("tensor", "pipe")),
            P(("groups", "dp"), ("tensor", "pipe")),
            P(("groups", "dp"), ("tensor", "pipe"), None),
            P(("groups", "dp"), None, ("tensor", "pipe")),
        ),
        check_vma=False,
    )
```

profile of v0, /device:TPU:16, one launch (start us, length us, event | category | flops | bytes accessed | tf_op | source)
XLA Modules:
  0.0 471.8 jit_solution(4640563735683466740)
XLA Ops:
  8.0 0.0 copy-start
  8.0 0.8 fusion.25
  8.8 4.5 reduce-window.6
  13.3 0.1 slice.12
  13.4 0.1 copy.27
  13.5 0.1 copy.28
  13.6 0.1 broadcast_add_fusion
  13.7 0.9 convert_reduce_fusion
  14.6 6.3 %scatter_custom_fusion.1 = bf16[1536,256]{1,0:T(8,128)(2,1)} fusion(s32[1024]{0:T(1024)S(1)} %bitcast.63, bf16[1024,256]{1,0:T(8,128)(2,1)} %param.11, bf16[]{:T(256)} %constant.10.clone.1), kind=kCustom, calls=%fused_computation.27 | custom fusion | bytes 786944 | tf_op jit(solution)/shard_map/scatter | solution.py:40
  20.9 5.2 %all-to-all-start.2 = ((bf16[4,4,96,256]{3,2,1,0:T(8,128)(2,1)}), bf16[4,4,96,256]{3,2,1,0:T(8,128)(2,1)S(1)}, u32[]{:S(2)}, u32[]{:S(2)}) async-start(bf16[4,4,96,256]{3,2,1,0:T(8,128)(2,1)} %bitcast.14), calls=%async_computation.3 | async-start | bytes 1572864 | tf_op jit(solution)/shard_map/all_to_all | solution.py:85
  26.1 11.2 %scatter_custom_fusion = bf16[1536,2048]{1,0:T(8,128)(2,1)} fusion(s32[1024]{0:T(1024)S(1)} %bitcast.64, bf16[1024,2048]{1,0:T(8,128)(2,1)} %param.7, bf16[]{:T(256)} %constant.10.clone.1), kind=kCustom, calls=%fused_computation.8 | custom fusion | bytes 6291968 | tf_op jit(solution)/shard_map/scatter | solution.py:40
  37.3 5.6 %all-to-all-done.2 = bf16[4,4,96,256]{3,2,1,0:T(8,128)(2,1)S(1)} async-done(((bf16[4,4,96,256]{3,2,1,0:T(8,128)(2,1)}), bf16[4,4,96,256]{3,2,1,0:T(8,128)(2,1)S(1)}, u32[]{:S(2)}, u32[]{:S(2)}) %all-to-all-start.2) | async-done | bytes 786464 | tf_op jit(solution)/shard_map/all_to_all | solution.py:85
  42.9 0.0 copy-start.3
  42.9 8.6 %all-to-all-start = ((bf16[4,4,96,2048]{3,2,1,0:T(8,128)(2,1)}), bf16[4,4,96,2048]{3,2,1,0:T(8,128)(2,1)}, u32[]{:S(2)}, u32[]{:S(2)}) async-start(bf16[4,4,96,2048]{3,2,1,0:T(8,128)(2,1)} %bitcast.57), calls=%async_computation.1 | async-start | bytes 12582912 | tf_op jit(solution)/shard_map/all_to_all | solution.py:63
  51.5 0.0 all-reduce.3.cloned.1.call-start
  51.5 0.0 copy-done.3
  51.5 1.1 fusion.9
  52.6 133.2 %all-to-all-done = bf16[4,4,96,2048]{3,2,1,0:T(8,128)(2,1)} async-done(((bf16[4,4,96,2048]{3,2,1,0:T(8,128)(2,1)}), bf16[4,4,96,2048]{3,2,1,0:T(8,128)(2,1)}, u32[]{:S(2)}, u32[]{:S(2)}) %all-to-all-start) | async-done | bytes 6291488 | tf_op jit(solution)/shard_map/all_to_all | solution.py:63
  185.8 0.0 copy-done
  185.8 5.9 %fusion.10 = bf16[4,4,96,64]{2,3,0,1:T(8,128)(2,1)} fusion(bf16[4,4,96,2048]{3,2,1,0:T(8,128)(2,1)} %all-to-all-done, bf16[4,2048,64]{1,2,0:T(8,128)(2,1)S(1)} %copy-done), kind=kOutput, calls=%fused_computation.18 | convolution fusion | flops 402751488 | bytes 7536640 | tf_op jit(solution)/shard_map/fuxn,unz->fuxz/dot_general | solution.py:65
  191.7 0.0 all-reduce.3.cloned.1.call-update
  191.7 0.0 all-gather.3.cloned.1.call-start
  191.8 0.5 all-gather.3.cloned.1.call-update
  192.3 34.7 %all-reduce.3.cloned.1.call-done = (bf16[4,4,96,64]{2,3,0,1:T(8,128)(2,1)}, bf16[4,4,96,64]{2,3,0,1:T(8,128)(2,1)}) async-done(((bf16[4,4,96,64]{2,3,0,1:T(8,128)(2,1)}, bf16[4,4,96,64]{2,3,0,1:T(8,128)(2,1)}), (bf16[4,4,96,64]{2,3,0,1:T(8,128)(2,1)}, bf16[4,4,96,64]{2,3,0,1:T(8,128)(2,1)})) %all-reduce.3.cloned.1.call-update) | async-done | bytes 393232 | tf_op jit(solution)/shard_map/psum | solution.py:64
  227.0 0.0 copy-start.2
  227.0 1.4 fusion.5
  228.5 0.9 copy.30
  229.4 5.1 %all-to-all-start.1 = ((bf16[4,4,96,256]{3,2,1,0:T(8,128)(2,1)}), bf16[4,4,96,256]{3,2,1,0:T(8,128)(2,1)S(1)}, u32[]{:S(2)}, u32[]{:S(2)}) async-start(bf16[4,4,96,256]{3,2,1,0:T(8,128)(2,1)} %copy.30), calls=%async_computation.2 | async-start | bytes 1572864 | tf_op jit(solution)/shard_map/all_to_all | solution.py:70
  234.5 0.0 copy-done.2
  234.5 1.8 convert_bitcast_fusion
  236.3 3.2 copy.32
  239.5 36.5 %all-to-all-done.1 = bf16[4,4,96,256]{3,2,1,0:T(8,128)(2,1)S(1)} async-done(((bf16[4,4,96,256]{3,2,1,0:T(8,128)(2,1)}), bf16[4,4,96,256]{3,2,1,0:T(8,128)(2,1)S(1)}, u32[]{:S(2)}, u32[]{:S(2)}) %all-to-all-start.1) | async-done | bytes 786464 | tf_op jit(solution)/shard_map/all_to_all | solution.py:70
  276.0 8.5 %all-to-all-start.3 = ((bf16[4,4,96,2048]{3,2,1,0:T(8,128)(2,1)}), bf16[4,4,96,2048]{3,2,1,0:T(8,128)(2,1)}, u32[]{:S(2)}, u32[]{:S(2)}) async-start(bf16[4,4,96,2048]{3,2,1,0:T(8,128)(2,1)} %copy.32), calls=%async_computation.4 | async-start | bytes 12582912 | tf_op jit(solution)/shard_map/all_to_all | solution.py:98
  284.5 0.0 copy-start.4
  284.5 0.0 copy-start.1
  284.5 0.0 reduce-scatter.2.cloned.1.call-start
  284.5 44.0 %all-gather.3.cloned.1.call-done = bf16[2048,1024]{1,0:T(8,128)(2,1)} async-done(((bf16[2048,256]{1,0:T(8,128)(2,1)}), bf16[2048,1024]{1,0:T(8,128)(2,1)}) %all-gather.3.cloned.1.call-update) | async-done | bytes 4194320 | tf_op jit(solution)/shard_map/all_gather | solution.py:49
  328.4 9.3 %convolution_convert_fusion = bf16[1024,1024]{1,0:T(8,128)(2,1)} fusion(bf16[1024,2048]{1,0:T(8,128)(2,1)} %param.7, bf16[2048,1024]{1,0:T(8,128)(2,1)} %all-gather.3.cloned.1.call-done), kind=kOutput, calls=%fused_computation.12 | convolution fusion | flops 4296015872 | bytes 10485760 | tf_op jit(solution)/shard_map/dot_general | solution.py:47
  337.7 0.0 reduce-scatter.2.cloned.1.call-update
  337.7 0.0 all-gather.5.cloned.1.call-start
  337.8 0.7 all-gather.5.cloned.1.call-update
  338.5 90.6 %psum.23 = f32[16]{0:T(128)S(1)} all-reduce(f32[16]{0:T(128)S(1)} %convert_element_type.77), channel_id=1, replica_groups=mesh['groups'=2,'dp'=4,'tensor'=2,'pipe'=2] {'dp'}, use_global_device_ids=true, to_apply=%region_10.11 | all-reduce | flops 16 | bytes 128 | tf_op jit(solution)/shard_map/psum | solution.py:30
  429.1 0.0 copy-done.4
  429.1 0.2 select_reduce_fusion.1
  429.3 0.0 copy-done.1
  429.3 1.0 fusion.13
  430.4 5.4 %fusion.4 = f32[4,2048,64]{1,2,0:T(8,128)} fusion(bf16[4,4,96,2048]{3,2,1,0:T(8,128)(2,1)} %all-to-all-done, f32[4]{0:T(128)S(1)} %get-tuple-element.10, bf16[4,4,96,64]{2,3,0,1:T(8,128)(2,1)S(1)} %copy-done.2), kind=kOutput, calls=%fused_computation.11 | convolution fusion | flops 403472384 | bytes 8585232 | tf_op jit(solution)/shard_map/sjmd,sjmr->jdr/dot_general | solution.py:111
  435.7 3.9 gather_fusion
  439.7 0.0 reduce-scatter.2.cloned.1.call-done
  439.7 2.0 add_convert_fusion.1
  441.7 0.0 all-to-all-done.3
  441.7 12.4 %gather_fusion.1 = bf16[1024,2048]{1,0:T(8,128)(2,1)} fusion(bf16[1536,2048]{1,0:T(8,128)(2,1)} %bitcast.19, s32[1024]{0:T(1024)S(1)} %broadcast_clamp_fusion), kind=kCustom, calls=%fused_computation.1 | custom fusion | bytes 8392704 | tf_op jit(solution)/shard_map/gather | solution.py:44
  454.1 0.0 all-gather.5.cloned.1.call-done
  454.1 10.6 %add_convert_fusion = bf16[1024,2048]{1,0:T(8,128)(2,1)} fusion(bf16[1024,2048]{1,0:T(8,128)(2,1)} %gather_fusion.1, bf16[1024,1024]{1,0:T(8,128)(2,1)} %all-gather.5.cloned.1.call-done, bf16[2048,1024]{1,0:T(8,128)(2,1)} %all-gather.3.cloned.1.call-done), kind=kOutput, calls=%fused_computation.4 | convolution fusion | flops 4301258752 | bytes 14680064 | tf_op jit(solution)/shard_map/dot_general | solution.py:52
  (8 shorter events, 0.1 us)
Async XLA Ops:
  8.0 177.8 %copy-start = (bf16[4,2048,64]{1,2,0:T(8,128)(2,1)S(1)}, bf16[4,2048,64]{1,2,0:T(8,128)(2,1)}, u32[]{:S(2)}) copy-start(bf16[4,2048,64]{1,2,0:T(8,128)(2,1)} %param.9) | copy-start | bytes 3145732
  20.9 22.0 %all-to-all-start.2 = ((bf16[4,4,96,256]{3,2,1,0:T(8,128)(2,1)}), bf16[4,4,96,256]{3,2,1,0:T(8,128)(2,1)S(1)}, u32[]{:S(2)}, u32[]{:S(2)}) async-start(bf16[4,4,96,256]{3,2,1,0:T(8,128)(2,1)} %bitcast.14), calls=%async_computation.3 | async-start | bytes 1572864 | tf_op jit(solution)/shard_map/all_to_all | solution.py:85
  42.9 8.6 %copy-start.3 = (bf16[4,64,256]{2,1,0:T(8,128)(2,1)S(1)}, bf16[4,64,256]{2,1,0:T(8,128)(2,1)}, u32[]{:S(2)}) copy-start(bf16[4,64,256]{2,1,0:T(8,128)(2,1)} %param.10) | copy-start | bytes 393220
  42.9 142.9 %all-to-all-start = ((bf16[4,4,96,2048]{3,2,1,0:T(8,128)(2,1)}), bf16[4,4,96,2048]{3,2,1,0:T(8,128)(2,1)}, u32[]{:S(2)}, u32[]{:S(2)}) async-start(bf16[4,4,96,2048]{3,2,1,0:T(8,128)(2,1)} %bitcast.57), calls=%async_computation.1 | async-start | bytes 12582912 | tf_op jit(solution)/shard_map/all_to_all | solution.py:63
  51.5 175.5 %all-reduce.3.cloned.1.call-start = ((), (), s32[]{:S(2)}) async-start(), calls=%async_computation.8 | async-start | bytes 1048576 | tf_op jit(solution)/shard_map/psum | solution.py:64
  191.7 136.7 %all-gather.3.cloned.1.call-start = ((), (), s32[]{:S(2)}) async-start(), calls=%async_computation.5 | async-start | bytes 5242880 | tf_op jit(solution)/shard_map/all_gather | solution.py:49
  227.0 7.5 %copy-start.2 = (bf16[4,4,96,64]{2,3,0,1:T(8,128)(2,1)S(1)}, bf16[4,4,96,64]{2,3,0,1:T(8,128)(2,1)}, u32[]{:S(2)}) copy-start(bf16[4,4,96,64]{2,3,0,1:T(8,128)(2,1)} %get-tuple-element.8) | copy-start | bytes 589828
  229.4 46.6 %all-to-all-start.1 = ((bf16[4,4,96,256]{3,2,1,0:T(8,128)(2,1)}), bf16[4,4,96,256]{3,2,1,0:T(8,128)(2,1)S(1)}, u32[]{:S(2)}, u32[]{:S(2)}) async-start(bf16[4,4,96,256]{3,2,1,0:T(8,128)(2,1)} %copy.30), calls=%async_computation.2 | async-start | bytes 1572864 | tf_op jit(solution)/shard_map/all_to_all | solution.py:70
  276.0 165.7 %all-to-all-start.3 = ((bf16[4,4,96,2048]{3,2,1,0:T(8,128)(2,1)}), bf16[4,4,96,2048]{3,2,1,0:T(8,128)(2,1)}, u32[]{:S(2)}, u32[]{:S(2)}) async-start(bf16[4,4,96,2048]{3,2,1,0:T(8,128)(2,1)} %copy.32), calls=%async_computation.4 | async-start | bytes 12582912 | tf_op jit(solution)/shard_map/all_to_all | solution.py:98
  284.5 144.7 %copy-start.4 = (s32[16]{0:T(128)S(1)}, s32[16]{0:T(128)}, u32[]{:S(2)}) copy-start(s32[16]{0:T(128)} %param.13) | copy-start | bytes 196
  284.5 144.9 %copy-start.1 = (bf16[4,4,96,64]{2,3,0,1:T(8,128)(2,1)S(1)}, bf16[4,4,96,64]{2,3,0,1:T(8,128)(2,1)}, u32[]{:S(2)}) copy-start(bf16[4,4,96,64]{2,3,0,1:T(8,128)(2,1)} %get-tuple-element.7) | copy-start | bytes 589828
  284.5 155.2 %reduce-scatter.2.cloned.1.call-start = ((), (), s32[]{:S(2)}) async-start(), calls=%async_computation.6 | async-start | bytes 2621440 | tf_op jit(solution)/shard_map/reduce_scatter | solution.py:58
  337.7 116.4 %all-gather.5.cloned.1.call-start = ((), (), s32[]{:S(2)}) async-start(), calls=%async_computation.7 | async-start | bytes 2621440 | tf_op jit(solution)/shard_map/all_gather | solution.py:46
Sparse Core Ops, SparseCore 0:
  191.9 35.1 all-reduce.2
  337.8 32.5 reduce-scatter.1
  372.1 22.8 all-gather.4
Sparse Core Ops, SparseCore 1:
  193.8 134.6 all-gather.2
where the time goes:
time: 472 us
  waiting for transfers between devices  255 us (54%)
  blocking collectives  90.6 us (19%)
  local copies, waits for them, and re-layouts  38.3 us (8%)
  matrix products  36.5 us (8%)
  starting transfers between devices  27.5 us (6%)
  between operations  15.3 us (3%)
  other arithmetic  8.46 us (2%)
    all_to_all x1, waiting for transfers between devices, local(): lax.all_to_all(send_x, 'dp', split_axis=0, concat_axis=0, tiled=True)  133 us
    psum x1, blocking collectives, local(): totals = lax.psum(jnp.sum(chosen, axis=0).astype(jnp.float32), 'dp')  90.6 us
    all_gather x1, waiting for transfers between devices, local(): lax.all_gather(frozen_value_weight, 'dp', axis=1, tiled=True)  44 us
    all_to_all x1, waiting for transfers between devices, local(): lax.all_to_all((adapter_scale * jnp.einsum('ykzl,klb->ykzb', rank_space_r...  36.5 us
    psum x1, waiting for transfers between devices, local(): lax.psum(jnp.einsum('fuxn,unz->fuxz', received_input, adapter_down_maps,...  34.7 us
    scatter x2, local copies, waits for them, and re-layouts, pack_rows(): buffer = buffer.at[position].set(token_rows)  17.5 us
    gather x2, local copies, waits for them, and re-layouts, restore_rows(): return buffer.reshape(adapters * slots_each, buffer.shape[3])[position]  16.3 us
    dot_general x1, matrix products, local(): lax.dot_general(grad_full, lax.all_gather(frozen_value_weight, 'dp', axis...  10.6 us
  transfers between devices with their start and end apart: 8, of which 5 were waited for; matrix products, arithmetic and copies ran while one was open for 11% of the time, Pallas kernels for 0%

commit v1 on v0

v1 whole, which is shorter than its diff:
```python
import jax
import jax.numpy as jnp
from jax import lax
from jax.sharding import PartitionSpec as P

adapter_scale = 2.0
TP = ("tensor", "pipe")


def dot(a, b, dims):
    return lax.dot_general(a, b, (dims, ((), ())), preferred_element_type=jnp.float32)


def local(acts, weight, down, up, dy, token_adapter, adapter_slot):
    per, feat, rank = down.shape
    cols = up.shape[2]
    tok = acts.shape[0]
    adapters = adapter_slot.shape[0]
    wide = adapters * rank
    fold = 2 * rank
    ids = token_adapter[:, 0]
    chosen = ids[:, None] == jnp.arange(adapters, dtype=jnp.int32)[None, :]
    slot_tok = jnp.sum(jnp.where(chosen, adapter_slot[None, :], 0), axis=1)
    slot_hot = slot_tok[:, None] == jnp.arange(adapters, dtype=jnp.int32)[None, :]
    counts = lax.psum(jnp.sum(slot_hot.astype(jnp.float32), axis=0), "dp")
    first = lax.axis_index("dp") * per
    own_counts = lax.dynamic_slice(counts, (first,), (per,))
    mask = slot_tok[:, None] == jnp.arange(wide, dtype=jnp.int32)[None, :] // rank

    def squeeze(full):
        full = jnp.where(mask, full, 0.0)
        return sum(full[:, i : i + fold] for i in range(0, wide, fold))

    def spread(rows):
        return jnp.where(mask, jnp.tile(rows, (1, wide // fold)), 0).astype(jnp.bfloat16)

    up_all = lax.all_gather(up.reshape(per * rank, cols), "dp", axis=0, tiled=True)
    down_all = lax.all_gather(
        down.transpose(1, 0, 2).reshape(feat, per * rank), "dp", axis=1, tiled=True
    )
    weight_all = lax.all_gather(weight, "dp", axis=1, tiled=True)
    dy_all = lax.all_gather(dy, TP, axis=1, tiled=True)

    grad_low = squeeze(dot(dy, up_all, ((1,), (1,)))).astype(jnp.bfloat16)
    grad_low = lax.psum(grad_low, TP).astype(jnp.float32) * adapter_scale
    grad_low = spread(grad_low.astype(jnp.bfloat16))
    part_down = dot(grad_low, acts, ((0,), (0,))).astype(jnp.bfloat16)
    sum_down = lax.psum_scatter(part_down, "dp", scatter_dimension=0, tiled=True)

    low = squeeze(dot(acts, down_all, ((1,), (0,)))).astype(jnp.bfloat16)
    low = spread(lax.psum(low, TP))
    part_up = dot(low, dy, ((0,), (0,))).astype(jnp.bfloat16)
    sum_up = lax.psum_scatter(part_up, "dp", scatter_dimension=0, tiled=True)
    delta = adapter_scale * dot(low, up_all, ((1,), (0,)))

    base = dot(acts, weight_all, ((1,), (0,))).astype(jnp.bfloat16)
    base = lax.psum_scatter(base, TP, scatter_dimension=1, tiled=True)
    layer_out = (base.astype(jnp.float32) + delta).astype(jnp.bfloat16)
    input_gradient = (
        dot(dy_all, weight_all, ((1,), (1,))) + dot(grad_low, down_all, ((1,), (1,)))
    ).astype(jnp.bfloat16)
    grad_down = sum_down.astype(jnp.float32).reshape(per, rank, feat).transpose(0, 2, 1)
    grad_down = grad_down * (1.0 / own_counts)[:, None, None]
    grad_up = sum_up.astype(jnp.float32).reshape(per, rank, cols)
    grad_up = grad_up * (adapter_scale / own_counts)[:, None, None]
    return (layer_out, input_gradient, grad_down, grad_up)


def solution(mesh):
    return jax.shard_map(
        local,
        mesh=mesh,
        in_specs=(
            P(("groups", "dp"), TP),
            P(TP, "dp"),
            P("dp", TP, None),
            P("dp", None, TP),
            P(("groups", "dp"), TP),
            P(("groups", "dp"), None),
            P(),
        ),
        out_specs=(
            P(("groups", "dp"), TP),
            P(("groups", "dp"), TP),
            P(("groups", "dp"), TP, None),
            P(("groups", "dp"), None, TP),
        ),
        check_vma=False,
    )
```

time: 472 us -> 386 us (0.82)
  the two profiles are of different devices: /device:TPU:16 before, /device:TPU:3 now
where the time goes in v1:
time: 386 us; the launch traced here: 384 us
  waiting for transfers between devices  292 us (76%)
  matrix products  46.1 us (12%)
  blocking collectives  21.8 us (6%)
  between operations  14.2 us (4%)
  other arithmetic  7.38 us (2%)
    all_gather x1, waiting for transfers between devices, local(): weight_all = lax.all_gather(weight, 'dp', axis=1, tiled=True)  81.1 us
    reduce_scatter x1, waiting for transfers between devices, local(): lax.psum_scatter(part_down, 'dp', scatter_dimension=0, tiled=True)  77.4 us
    all_gather x1, waiting for transfers between devices, local(): lax.all_gather(down.transpose(1, 0, 2).reshape(feat, per * rank), 'dp', a...  67 us
    dot_general x8, matrix products, dot(): lax.dot_general(a, b, (dims, ((), ())), preferred_element_type=jnp.float32)  46.1 us
    reduce_scatter x1, waiting for transfers between devices, local(): base = lax.psum_scatter(base, TP, scatter_dimension=1, tiled=True)  31.8 us
    psum x1, waiting for transfers between devices, local(): low = spread(lax.psum(low, TP))  28.6 us
    all_gather x1, blocking collectives, local(): lax.all_gather(up.reshape(per * rank, cols), 'dp', axis=0, tiled=True)  14.7 us
  transfers between devices with their start and end apart: 7, of which 6 were waited for; matrix products, arithmetic and copies ran while one was open for 11% of the time, Pallas kernels for 0%

profile of v1, /device:TPU:3, one launch (start us, length us, event | category | flops | bytes accessed | tf_op | source)
XLA Modules:
  0.0 384.3 jit_solution(7991623737874280773)
XLA Ops:
  7.2 0.0 all-gather.6.cloned.1.call-start
  7.2 0.7 all-gather.6.cloned.1.call-update
  7.9 0.0 all-reduce.3.cloned.1.call-start
  8.0 0.8 select_reduce_fusion
  8.7 14.7 %all_gather.14 = bf16[1024,256]{1,0:T(8,128)(2,1)S(1)} all-gather(bf16[256,256]{1,0:T(8,128)(2,1)} %bitcast.39), channel_id=1, replica_groups=mesh['groups'=2,'dp'=4,'tensor'=2,'pipe'=2] {'dp'}, dimensions={0}, use_global_device_ids=true | all-gather | bytes 655360 | tf_op jit(solution)/shard_map/all_gather | solution.py:37
  23.4 1.8 compare_select_fusion.1
  25.2 0.9 fusion.3
  26.1 67.0 %all-gather.6.cloned.1.call-done = bf16[2048,1024]{0,1:T(8,128)(2,1)} async-done(((bf16[2048,256]{0,1:T(8,128)(2,1)}), bf16[2048,1024]{0,1:T(8,128)(2,1)}) %all-gather.6.cloned.1.call-update) | async-done | bytes 4194320 | tf_op jit(solution)/shard_map/all_gather | solution.py:38
  93.2 7.6 %compare_select_fusion.3 = f32[1024,1024]{1,0:T(8,128)S(1)} fusion(s32[1024]{0:T(1024)S(1)} %add_select_fusion, s32[1024]{0:T(1024)S(1)} %select_reduce_fusion, bf16[1024,2048]{1,0:T(8,128)(2,1)} %param.7, bf16[2048,1024]{0,1:T(8,128)(2,1)} %all-gather.6.cloned.1.call-done), kind=kOutput, calls=%fused_computation.4 | convolution fusion | flops 4297064448 | bytes 12591104 | tf_op jit(solution)/shard_map/dot_general | solution.py:11
  100.7 0.0 copy-start
  100.8 0.9 fusion.4
  101.7 0.0 all-reduce.3.cloned.1.call-update
  101.7 0.0 all-gather.4.cloned.1.call-start
  101.7 0.7 all-gather.4.cloned.1.call-update
  102.4 0.0 all-gather.8.cloned.1.call-start
  102.5 0.5 all-gather.8.cloned.1.call-update
  103.0 0.0 reduce-scatter.8.cloned.1.call-start
  103.0 28.6 %all-reduce.3.cloned.1.call-done = (bf16[1024,128]{1,0:T(8,128)(2,1)}, bf16[1024,128]{1,0:T(8,128)(2,1)}) async-done(((bf16[1024,128]{1,0:T(8,128)(2,1)}, bf16[1024,128]{1,0:T(8,128)(2,1)}), (bf16[1024,128]{1,0:T(8,128)(2,1)}, bf16[1024,128]{1,0:T(8,128)(2,1)})) %all-reduce.3.cloned.1.call-update) | async-done | bytes 524304 | tf_op jit(solution)/shard_map/psum | solution.py:51
  131.6 1.2 tile.8
  132.9 0.0 copy-done
  132.9 1.9 convolution_convert_fusion.2
  134.8 0.0 reduce-scatter.8.cloned.1.call-update
  134.8 0.0 copy-start.3
  134.8 0.0 reduce-scatter.4.cloned.1.call-start
  134.9 81.1 %all-gather.4.cloned.1.call-done = bf16[2048,1024]{1,0:T(8,128)(2,1)} async-done(((bf16[2048,256]{1,0:T(8,128)(2,1)}), bf16[2048,1024]{1,0:T(8,128)(2,1)}) %all-gather.4.cloned.1.call-update) | async-done | bytes 4194320 | tf_op jit(solution)/shard_map/all_gather | solution.py:41
  216.0 9.3 %convolution_convert_fusion.1 = bf16[1024,1024]{1,0:T(8,128)(2,1)} fusion(bf16[1024,2048]{1,0:T(8,128)(2,1)} %param.7, bf16[2048,1024]{1,0:T(8,128)(2,1)} %all-gather.4.cloned.1.call-done), kind=kOutput, calls=%fused_computation.8 | convolution fusion | flops 4296015872 | bytes 10485760 | tf_op jit(solution)/shard_map/dot_general | solution.py:11
  225.2 0.0 reduce-scatter.4.cloned.1.call-update
  225.3 0.0 reduce-scatter.6.cloned.1.call-start
  225.3 0.0 copy-done.3
  225.3 0.1 multiply_convert_fusion
  225.4 0.3 tile.20
  225.7 0.0 copy-start.1
  225.7 1.3 copy-done.1
  227.0 8.8 %convolution_convert_fusion = bf16[1024,2048]{1,0:T(8,128)(2,1)} fusion(bf16[1024,2048]{1,0:T(8,128)(2,1)} %param.7, bf16[128,8,8,128]{3,2,1,0:T(8,128)(2,1)S(1)} %bitcast.35, s32[1024]{0:T(1024)S(1)} %add_select_fusion, s32[1024]{0:T(1024)S(1)} %select_reduce_fusion), kind=kOutput, calls=%fused_computation.5 | convolution fusion | flops 4299161600 | bytes 10493952 | tf_op jit(solution)/shard_map/dot_general | solution.py:11
  235.7 0.0 reduce-scatter.6.cloned.1.call-update
  235.8 0.1 convert_reduce_fusion
  235.9 7.1 %psum.23 = f32[16]{0:T(128)S(1)} all-reduce(f32[16]{0:T(128)S(1)} %convert_reduce_fusion), channel_id=1, replica_groups=mesh['groups'=2,'dp'=4,'tensor'=2,'pipe'=2] {'dp'}, use_global_device_ids=true, to_apply=%region_6.7 | all-reduce | flops 16 | bytes 128 | tf_op jit(solution)/shard_map/psum | solution.py:25
  243.0 0.1 broadcast_divide_fusion
  243.1 0.0 all-gather.8.cloned.1.call-done
  243.1 0.0 copy-start.2
  243.1 0.0 copy-start.4
  243.1 7.2 %fusion.12 = f32[1024,2048]{1,0:T(8,128)S(1)} fusion(bf16[1024,1024]{1,0:T(8,128)(2,1)} %all-gather.8.cloned.1.call-done, bf16[2048,1024]{1,0:T(8,128)(2,1)} %all-gather.4.cloned.1.call-done), kind=kOutput, calls=%fused_computation.48 | convolution fusion | flops 4294967296 | bytes 14680064 | tf_op jit(solution)/shard_map/dot_general | solution.py:11
  250.3 0.0 copy-done.2
  250.3 0.0 copy-done.4
  250.3 6.8 %add_convert_fusion = bf16[1024,2048]{1,0:T(8,128)(2,1)} fusion(f32[1024,2048]{1,0:T(8,128)S(1)} %fusion.12, bf16[2048,1024]{0,1:T(8,128)(2,1)S(1)} %copy-done.4, bf16[128,8,8,128]{3,2,1,0:T(8,128)(2,1)S(1)} %bitcast.36, s32[1024]{0:T(1024)S(1)} %add_select_fusion, s32[1024]{0:T(1024)S(1)} %select_reduce_fusion), kind=kOutput, calls=%fused_computation | convolution fusion | flops 4301258752 | bytes 18882560 | tf_op jit(solution)/shard_map/dot_general | solution.py:11
  257.0 3.8 reduce-scatter.8.cloned.1.call-done
  260.8 1.7 convert_multiply_fusion.1
  262.5 31.8 %reduce-scatter.4.cloned.1.call-done = bf16[1024,256]{1,0:T(8,128)(2,1)} async-done(((bf16[1024,1024]{1,0:T(8,128)(2,1)}), bf16[1024,256]{1,0:T(8,128)(2,1)}) %reduce-scatter.4.cloned.1.call-update) | async-done | bytes 524304 | tf_op jit(solution)/shard_map/reduce_scatter | solution.py:57
  294.3 2.9 fusion.2
  297.2 77.4 %reduce-scatter.6.cloned.1.call-done = bf16[256,2048]{1,0:T(8,128)(2,1)} async-done(((bf16[1024,2048]{1,0:T(8,128)(2,1)}), bf16[256,2048]{1,0:T(8,128)(2,1)}) %reduce-scatter.6.cloned.1.call-update) | async-done | bytes 1048592 | tf_op jit(solution)/shard_map/reduce_scatter | solution.py:48
  374.6 2.9 fusion
  (1 shorter events, 0.0 us)
Async XLA Ops:
  7.2 86.0 %all-gather.6.cloned.1.call-start = ((), (), s32[]{:S(2)}) async-start(), calls=%async_computation.5 | async-start | bytes 5242880 | tf_op jit(solution)/shard_map/all_gather | solution.py:38
  7.9 123.7 %all-reduce.3.cloned.1.call-start = ((), (), s32[]{:S(2)}) async-start(), calls=%async_computation.9 | async-start | bytes 1048576 | tf_op jit(solution)/shard_map/psum | solution.py:51
  100.7 32.1 %copy-start = (bf16[1024,256]{1,0:T(8,128)(2,1)S(1)}, bf16[1024,256]{1,0:T(8,128)(2,1)}, u32[]{:S(2)}) copy-start(bf16[1024,256]{1,0:T(8,128)(2,1)} %param.11) | copy-start | bytes 1572868
  101.7 114.3 %all-gather.4.cloned.1.call-start = ((), (), s32[]{:S(2)}) async-start(), calls=%async_computation.3 | async-start | bytes 5242880 | tf_op jit(solution)/shard_map/all_gather | solution.py:41
  102.4 140.7 %all-gather.8.cloned.1.call-start = ((), (), s32[]{:S(2)}) async-start(), calls=%async_computation.6 | async-start | bytes 2621440 | tf_op jit(solution)/shard_map/all_gather | solution.py:42
  103.0 157.8 %reduce-scatter.8.cloned.1.call-start = ((), (), s32[]{:S(2)}) async-start(), calls=%async_computation.8 | async-start | bytes 655360 | tf_op jit(solution)/shard_map/reduce_scatter | solution.py:53
  134.8 90.5 %copy-start.3 = (bf16[1024,128]{1,0:T(8,128)(2,1)S(1)}, bf16[1024,128]{1,0:T(8,128)(2,1)}, u32[]{:S(2)}) copy-start(bf16[1024,128]{1,0:T(8,128)(2,1)} %get-tuple-element.5) | copy-start | bytes 786436
  134.8 159.5 %reduce-scatter.4.cloned.1.call-start = ((), (), s32[]{:S(2)}) async-start(), calls=%async_computation.4 | async-start | bytes 2621440 | tf_op jit(solution)/shard_map/reduce_scatter | solution.py:57
  225.3 149.3 %reduce-scatter.6.cloned.1.call-start = ((), (), s32[]{:S(2)}) async-start(), calls=%async_computation.7 | async-start | bytes 5242880 | tf_op jit(solution)/shard_map/reduce_scatter | solution.py:48
  225.7 1.3 copy-start.1
  243.1 7.2 %copy-start.2 = (bf16[1024,8,128]{2,1,0:T(8,128)(2,1)S(1)}, bf16[1024,8,128]{2,1,0:T(8,128)(2,1)}, u32[]{:S(2)}) copy-start(bf16[1024,8,128]{2,1,0:T(8,128)(2,1)} %copy-done.1) | copy-start | bytes 6291460
  243.1 7.2 %copy-start.4 = (bf16[2048,1024]{0,1:T(8,128)(2,1)S(1)}, bf16[2048,1024]{0,1:T(8,128)(2,1)}, u32[]{:S(2)}) copy-start(bf16[2048,1024]{0,1:T(8,128)(2,1)} %all-gather.6.cloned.1.call-done) | copy-start | bytes 12582916
Sparse Core Ops, SparseCore 0:
  9.6 83.5 all-gather.5
  101.8 29.7 all-reduce.2
  133.2 82.7 all-gather.3
  217.4 20.0 all-gather.7
  240.2 20.6 reduce-scatter.7
  263.8 30.5 reduce-scatter.3
  296.7 77.7 reduce-scatter.5

commit v2 on v1

--- a/solution.py
+++ b/solution.py
@@ -1,6 +1,10 @@
+import functools
+
 import jax
 import jax.numpy as jnp
 from jax import lax
+from jax.experimental import pallas as pl
+from jax.experimental.pallas import tpu as pltpu
 from jax.sharding import PartitionSpec as P
 
 adapter_scale = 2.0
@@ -11,7 +15,7 @@
     return lax.dot_general(a, b, (dims, ((), ())), preferred_element_type=jnp.float32)
 
 
-def local(acts, weight, down, up, dy, token_adapter, adapter_slot):
+def plain(acts, weight, down, up, dy, token_adapter, adapter_slot):
     per, feat, rank = down.shape
     cols = up.shape[2]
     tok = acts.shape[0]
@@ -66,9 +70,549 @@
     return (layer_out, input_gradient, grad_down, grad_up)
 
 
+LANES = 128
+ROWS = 256
+
+
+def fused_kernel(
+    sizes,
+    x_hbm, a_hbm, w_hbm, b_hbm, dy_hbm, slot_col, slot_row, cnt_ref,
+    out_ref, ig_ref, down_ref, up_ref, cnt_out,
+    x, a_all, w_all, b_all, dy_all, part, recv_r, recv_l, base_send, base_recv, acc,
+    fold, grad_low, low, grad_t, lhs, gpack_send, gpack_recv, lpack_send, lpack_recv,
+    up_send, up_recv, cnt_recv,
+    load_sem, b_ss, b_rs, c_ss, c_rs, az_ss, az_rs, ay_ss, ay_rs, wz_ss, wz_rs, wy_ss, wy_rs,
+    dy_ss, dy_rs, g_ss, g_rs, l_ss, l_rs, rs_ss, rr_rs, rl_rs, base_ss, base_rs, up_ss, up_rs,
+):
+    depth, pipes, peers, per, rank = sizes
+    tok, feat = x.shape
+    wide = per * rank
+    pieces = wide // LANES
+    each = LANES // rank
+    i = lax.axis_index("dp")
+    g = lax.axis_index("groups")
+    k = lax.axis_index("tensor") * pipes + lax.axis_index("pipe")
+    half = feat // 2
+    mine = pl.ds(pl.multiple_of(g * half, half), half)
+    other = pl.ds(pl.multiple_of((1 - g) * half, half), half)
+    y_dev = {"groups": 1 - g}
+
+    def tp_dev(kk):
+        return {"tensor": kk // pipes, "pipe": kk % pipes}
+
+    def rc(src, dst, ss, rs, dev):
+        return pltpu.make_async_remote_copy(
+            src_ref=src, dst_ref=dst, send_sem=ss, recv_sem=rs,
+            device_id=dev, device_id_type=pl.DeviceIdType.MESH,
+        )
+
+    loads = [
+        pltpu.make_async_copy(b_hbm, b_all.at[i], load_sem.at[0]),
+        pltpu.make_async_copy(a_hbm, a_all.at[i], load_sem.at[1]),
+        pltpu.make_async_copy(x_hbm, x, load_sem.at[2]),
+        pltpu.make_async_copy(w_hbm, w_all.at[i], load_sem.at[3]),
+        pltpu.make_async_copy(dy_hbm, dy_all.at[k], load_sem.at[4]),
+    ]
+    for c in loads:
+        c.start()
+
+    barrier = pltpu.get_barrier_semaphore()
+    for q in range(1, depth):
+        pl.semaphore_signal(barrier, inc=1, device_id={"dp": (i + q) % depth},
+                            device_id_type=pl.DeviceIdType.MESH)
+    for q in range(1, peers):
+        pl.semaphore_signal(barrier, inc=1, device_id=tp_dev((k + q) % peers),
+                            device_id_type=pl.DeviceIdType.MESH)
+    pl.semaphore_signal(barrier, inc=1, device_id=y_dev, device_id_type=pl.DeviceIdType.MESH)
+    pl.semaphore_wait(barrier, depth + peers - 1)
+
+    def b_copy(j, src):
+        return rc(b_all.at[src], b_all.at[src], b_ss.at[j], b_rs.at[src], {"dp": j})
+
+    def c_copy(j, src):
+        return rc(cnt_ref.at[j], cnt_recv.at[src], c_ss.at[j], c_rs.at[src], {"dp": j})
+
+    def tp_copy(send, recv, ss, rs, kk, src):
+        return rc(send, recv.at[src], ss.at[kk], rs.at[src], tp_dev(kk))
+
+    def dy_copy(kk, src):
+        return rc(dy_all.at[src], dy_all.at[src], dy_ss.at[kk], dy_rs.at[src], tp_dev(kk))
+
+    def z_copy(buf, ss, rs, src, way, to):
+        ref = buf.at[src, mine]
+        return rc(ref, ref, ss.at[way, src], rs.at[src], {"dp": to})
+
+    def y_copy(buf, ss, rs, src, rows):
+        ref = buf.at[src, rows]
+        return rc(ref, ref, ss.at[src], rs.at[src], y_dev)
+
+    def own_sends(buf, ss, rs):
+        @pl.when(i > 0)
+        def _():
+            z_copy(buf, ss, rs, i, 1, i - 1).start()
+
+        @pl.when(i < depth - 1)
+        def _():
+            z_copy(buf, ss, rs, i, 0, i + 1).start()
+
+    def ways(s, body):
+        def step(way, carry):
+            src = i + (2 * way - 1) * s
+
+            @pl.when((src >= 0) & (src < depth))
+            def _():
+                body(src, way)
+
+            return carry
+
+        lax.fori_loop(0, 2, step, 0)
+
+    def forward(buf, zs, zr, ys, yr, s):
+        def body(src, way):
+            to = i + 1 - 2 * way
+            z_copy(buf, zs, zr, src, way, (i + 1) % depth).wait_recv()
+
+            @pl.when((to >= 0) & (to < depth))
+            def _():
+                z_copy(buf, zs, zr, src, way, to).start()
+
+            y_copy(buf, ys, yr, src, mine).start()
+
+        ways(s, body)
+
+    def drain(buf, zs, zr, ys, yr):
+        @pl.when(i > 0)
+        def _():
+            z_copy(buf, zs, zr, i, 1, i - 1).wait_send()
+
+        @pl.when(i < depth - 1)
+        def _():
+            z_copy(buf, zs, zr, i, 0, i + 1).wait_send()
+
+        for s in range(1, depth):
+
+            def body(src, way):
+                to = i + 1 - 2 * way
+
+                @pl.when((to >= 0) & (to < depth))
+                def _():
+                    z_copy(buf, zs, zr, src, way, to).wait_send()
+
+                y_copy(buf, ys, yr, src, mine).wait_send()
+
+            ways(s, body)
+
+    lane_slot = lax.broadcasted_iota(jnp.int32, (ROWS, LANES), 1) // rank
+    low_lanes = lax.broadcasted_iota(jnp.int32, (tok // 2, LANES), 1) < LANES // 2
+
+    def tiles(n, body):
+        def step(t, carry):
+            body(t)
+            return carry
+
+        lax.fori_loop(0, n, step, 0)
+
+    def rows_at(t, size=ROWS):
+        return pl.ds(pl.multiple_of(t * size, size), size)
+
+    def folded(z, j, rows):
+        total = None
+        for p in range(pieces):
+            hit = slot_col[rows, :] == lane_slot + (per * j + each * p)
+            term = jnp.where(hit, z[:, p * LANES : (p + 1) * LANES], 0.0)
+            total = term if total is None else total + term
+        return total
+
+    def spread(values, j, rows):
+        v = values[rows, :]
+        out = [
+            jnp.where(slot_col[rows, :] == lane_slot + (per * j + each * p), v, 0.0)
+            for p in range(pieces)
+        ]
+        return jnp.concatenate(out, axis=1).astype(jnp.bfloat16)
+
+    def transposed(values_t, j):
+        for p in range(pieces):
+            row_slot = lax.broadcasted_iota(jnp.int32, (LANES, tok), 0) // rank
+            hit = slot_row[0:1, :] == row_slot + (per * j + each * p)
+            lhs[p * LANES : (p + 1) * LANES, :] = jnp.where(hit, values_t[...], 0.0).astype(
+                jnp.bfloat16
+            )
+
+    def pack(dst):
+        f = fold[...]
+        f = f + pltpu.roll(f, LANES // 2, 1)
+        dst[...] = jnp.where(low_lanes, f[: tok // 2], f[tok // 2 :]).astype(jnp.bfloat16)
+
+    def unpack(send, recv, ss, rs, dst, scale):
+        total = send[...].astype(jnp.float32)
+        for q in range(1, peers):
+            kk = (k + q) % peers
+            tp_copy(send, recv, ss, rs, kk, kk).wait_recv()
+            total = total + recv[kk].astype(jnp.float32)
+        total = (scale * total).astype(jnp.bfloat16).astype(jnp.float32)
+        turned = pltpu.roll(total, LANES // 2, 1)
+        dst[: tok // 2, :] = jnp.where(low_lanes, total, turned)
+        dst[tok // 2 :, :] = jnp.where(low_lanes, turned, total)
+
+    def low_add(j):
+        def body(t):
+            rows = rows_at(t)
+            z = dot(x[rows, :], a_all[j], ((1,), (0,)))
+            fold[rows, :] = fold[rows, :] + folded(z, j, rows)
+
+        tiles(tok // ROWS, body)
+
+    def base_block(j):
+        def body(t):
+            rows = rows_at(t)
+            base_send[j, rows, :] = dot(x[rows, :], w_all[j], ((1,), (0,))).astype(jnp.bfloat16)
+
+        tiles(tok // ROWS, body)
+
+        @pl.when(j != k)
+        def _():
+            base_copy(j, k).start()
+
+    def base_copy(j, src):
+        return rc(base_send.at[j], base_recv.at[src], base_ss.at[j], base_rs.at[src], tp_dev(j))
+
+    wide_cols = 512
+
+    def back_a(j, first):
+        def body(t):
+            rows = rows_at(t)
+            left = spread(grad_low, j, rows)
+
+            def inner(c):
+                cols = rows_at(c, wide_cols)
+                z = dot(left, a_all[j, cols, :], ((1,), (1,)))
+                acc[rows, cols] = z if first else acc[rows, cols] + z
+
+            tiles(feat // wide_cols, inner)
+
+        tiles(tok // ROWS, body)
+
+    def back_w(j):
+        def body(t):
+            rows = rows_at(t)
+
+            def inner(c):
+                cols = rows_at(c, wide_cols)
+                z = dot(dy_all[j, rows, :], w_all[j, cols, :], ((1,), (1,)))
+                acc[rows, cols] = acc[rows, cols] + z
+
+            tiles(feat // wide_cols, inner)
+
+        tiles(tok // ROWS, body)
+
+    def make_part(d):
+        transposed(grad_t, d)
+
+        def body(c):
+            cols = rows_at(c, wide_cols)
+            part[d, :, cols] = dot(lhs[...], x[:, cols], ((1,), (0,))).astype(jnp.bfloat16)
+
+        tiles(feat // wide_cols, body)
+
+    def add_to_part(d, recv):
+        def body(c):
+            cols = rows_at(c, wide_cols)
+            total = part[d, :, cols].astype(jnp.float32) + recv[d, :, cols].astype(jnp.float32)
+            part[d, :, cols] = total.astype(jnp.bfloat16)
+
+        tiles(feat // wide_cols, body)
+
+    def rs_up(d, to):
+        return rc(part.at[d], recv_r.at[d], rs_ss.at[d], rr_rs.at[d], {"dp": to})
+
+    def rs_down(d, to):
+        return rc(part.at[d], recv_l.at[d], rs_ss.at[d], rl_rs.at[d], {"dp": to})
+
+    def reduce_step(t):
+        @pl.when(t >= i)
+        def _():
+            d = depth - 1 - t + i
+            make_part(d)
+
+            @pl.when(i > 0)
+            def _():
+                rs_up(d, i + 1).wait_recv()
+                add_to_part(d, recv_r)
+
+            rs_up(d, i + 1).start()
+
+        @pl.when(t >= depth - 1 - i)
+        def _():
+            d = i - (depth - 1 - t)
+            make_part(d)
+
+            @pl.when(i < depth - 1)
+            def _():
+                rs_down(d, i - 1).wait_recv()
+                add_to_part(d, recv_l)
+
+            rs_down(d, i - 1).start()
+
+    loads[0].wait()
+    for q in range(1, depth):
+        b_copy((i + q) % depth, i).start()
+    for q in range(1, depth):
+        c_copy((i + q) % depth, i).start()
+    loads[1].wait()
+    own_sends(a_all, az_ss, az_rs)
+    loads[2].wait()
+    loads[3].wait()
+    base_block(i)
+
+    loads[4].wait()
+    fold[...] = jnp.zeros_like(fold)
+
+    def grad_low_add(j):
+        def body(t):
+            rows = rows_at(t)
+            z = dot(dy_all[k, rows, :], b_all[j], ((1,), (1,)))
+            fold[rows, :] = fold[rows, :] + folded(z, j, rows)
+
+        tiles(tok // ROWS, body)
+
+    grad_low_add(i)
+
+    def b_step(q, carry):
+        j = (i + q) % depth
+        b_copy(j, j).wait_recv()
+        grad_low_add(j)
+        return carry
+
+    lax.fori_loop(1, depth, b_step, 0)
+    pack(gpack_send)
+    for q in range(1, peers):
+        tp_copy(gpack_send, gpack_recv, g_ss, g_rs, (k + q) % peers, k).start()
+    for q in range(1, peers):
+        dy_copy((k + q) % peers, k).start()
+    fold[...] = jnp.zeros_like(fold)
+    low_add(i)
+    unpack(gpack_send, gpack_recv, g_ss, g_rs, grad_low, adapter_scale)
+    grad_t[...] = jnp.transpose(grad_low[...])
+
+    def use_a(src, way):
+        y_copy(a_all, ay_ss, ay_rs, src, other).wait_recv()
+        low_add(src)
+        back_a(src, False)
+
+    for t in range(depth - 1):
+        reduce_step(t)
+        forward(a_all, az_ss, az_rs, ay_ss, ay_rs, t + 1)
+        if t == 0:
+            own_sends(w_all, wz_ss, wz_rs)
+            back_a(i, True)
+        else:
+            ways(t, use_a)
+    forward(w_all, wz_ss, wz_rs, wy_ss, wy_rs, 1)
+    ways(depth - 1, use_a)
+    pack(lpack_send)
+    for q in range(1, peers):
+        tp_copy(lpack_send, lpack_recv, l_ss, l_rs, (k + q) % peers, k).start()
+    for q in range(1, peers):
+        kk = (k + q) % peers
+        dy_copy(kk, kk).wait_recv()
+    back_w(i)
+    unpack(lpack_send, lpack_recv, l_ss, l_rs, low, 1.0)
+    grad_t[...] = jnp.transpose(low[...])
+
+    def up_copy(j, src):
+        return rc(up_send.at[j], up_recv.at[src], up_ss.at[j], up_rs.at[src], {"dp": j})
+
+    def up_part(q, carry):
+        j = (i + q) % depth
+        transposed(grad_t, j)
+        up_send[j] = dot(lhs[...], dy_all[k], ((1,), (0,))).astype(jnp.bfloat16)
+
+        @pl.when(q < depth)
+        def _():
+            up_copy(j, i).start()
+
+        return carry
+
+    lax.fori_loop(1, depth + 1, up_part, 0)
+
+    def use_w(src, way):
+        y_copy(w_all, wy_ss, wy_rs, src, other).wait_recv()
+        base_block(src)
+        back_w(src)
+
+    for s in range(2, depth):
+        forward(w_all, wz_ss, wz_rs, wy_ss, wy_rs, s)
+        ways(s - 1, use_w)
+
+    grad_t[...] = jnp.transpose(grad_low[...])
+    make_part(i)
+
+    @pl.when(i > 0)
+    def _():
+        rs_up(i, (i + 1) % depth).wait_recv()
+        add_to_part(i, recv_r)
+
+    @pl.when(i < depth - 1)
+    def _():
+        rs_down(i, (i + 1) % depth).wait_recv()
+        add_to_part(i, recv_l)
+
+    def down_out(c):
+        cols = rows_at(c, wide_cols)
+        down_ref[:, cols] = part[i, :, cols].astype(jnp.float32)
+
+    tiles(feat // wide_cols, down_out)
+
+    ways(depth - 1, use_w)
+
+    total = up_send[i].astype(jnp.float32)
+    cnt = cnt_ref[i]
+    for q in range(1, depth):
+        j = (i + q) % depth
+        up_copy(j, j).wait_recv()
+        total = total + up_recv[j].astype(jnp.float32)
+        c_copy(j, j).wait_recv()
+        cnt = cnt + cnt_recv[j]
+    up_ref[...] = total
+    cnt_out[...] = cnt
+
+    def ig_out(t):
+        rows = rows_at(t, 64)
+        ig_ref[rows, :] = acc[rows, :].astype(jnp.bfloat16)
+
+    tiles(tok // 64, ig_out)
+
+    for q in range(1, peers):
+        kk = (k + q) % peers
+        base_copy(kk, kk).wait_recv()
+
+    def finish(t):
+        rows = rows_at(t)
+        delta = None
+        for j in range(depth):
+            z = dot(spread(low, j, rows), b_all[j], ((1,), (0,)))
+            delta = z if delta is None else delta + z
+        delta = (adapter_scale * delta).astype(jnp.bfloat16).astype(jnp.float32)
+        base = base_send[k, rows, :].astype(jnp.float32)
+        for q in range(1, peers):
+            base = base + base_recv[(k + q) % peers, rows, :].astype(jnp.float32)
+        out_ref[rows, :] = (base + delta).astype(jnp.bfloat16)
+
+    tiles(tok // ROWS, finish)
+
+    drain(a_all, az_ss, az_rs, ay_ss, ay_rs)
+    drain(w_all, wz_ss, wz_rs, wy_ss, wy_rs)
+    for q in range(1, depth):
+        j = (i + q) % depth
+        b_copy(j, i).wait_send()
+        c_copy(j, i).wait_send()
+        up_copy(j, i).wait_send()
+        rs_up(j, j).wait_send()
+    for q in range(1, peers):
+        kk = (k + q) % peers
+        tp_copy(gpack_send, gpack_recv, g_ss, g_rs, kk, k).wait_send()
+        tp_copy(lpack_send, lpack_recv, l_ss, l_rs, kk, k).wait_send()
+        dy_copy(kk, k).wait_send()
+        base_copy(kk, k).wait_send()
+
+
+def fused(mesh_sizes, acts, weight, down, up, dy, token_adapter, adapter_slot):
+    depth, pipes, peers = mesh_sizes
+    per, feat, rank = down.shape
+    cols = up.shape[2]
+    tok = acts.shape[0]
+    adapters = adapter_slot.shape[0]
+    wide = per * rank
+    ids = token_adapter[:, 0]
+    everyone = jnp.arange(adapters, dtype=jnp.int32)
+    slot_tok = jnp.sum(jnp.where(ids[:, None] == everyone[None, :], adapter_slot[None, :], 0), axis=1)
+    counts = jnp.sum((slot_tok[:, None] == everyone[None, :]).astype(jnp.float32), axis=0)
+    cnt = jnp.broadcast_to(jnp.repeat(counts, rank).reshape(depth, 1, wide), (depth, 8, wide))
+    slot_col = jnp.broadcast_to(slot_tok[:, None], (tok, LANES))
+    slot_row = jnp.broadcast_to(slot_tok[None, :], (8, tok))
+    a = down.transpose(1, 0, 2).reshape(feat, wide)
+    b = up.reshape(wide, cols)
+    bf, f32 = jnp.bfloat16, jnp.float32
+    dma = pltpu.SemaphoreType.DMA
+    vmem = pl.BlockSpec(memory_space=pltpu.VMEM)
+    hbm = pl.BlockSpec(memory_space=pl.ANY)
+    layer_out, ig, sum_down, sum_up, total = pl.pallas_call(
+        functools.partial(fused_kernel, (depth, pipes, peers, per, rank)),
+        out_shape=(
+            jax.ShapeDtypeStruct((tok, cols), bf),
+            jax.ShapeDtypeStruct((tok, feat), bf),
+            jax.ShapeDtypeStruct((wide, feat), f32),
+            jax.ShapeDtypeStruct((wide, cols), f32),
+            jax.ShapeDtypeStruct((8, wide), f32),
+        ),
+        in_specs=[hbm] * 5 + [vmem] * 3,
+        out_specs=(vmem,) * 5,
+        scratch_shapes=[
+            pltpu.VMEM((tok, feat), bf),
+            pltpu.VMEM((depth, feat, wide), bf),
+            pltpu.VMEM((depth, feat, cols), bf),
+            pltpu.VMEM((depth, wide, cols), bf),
+            pltpu.VMEM((peers, tok, cols), bf),
+            pltpu.VMEM((depth, wide, feat), bf),
+            pltpu.VMEM((depth, wide, feat), bf),
+            pltpu.VMEM((depth, wide, feat), bf),
+            pltpu.VMEM((peers, tok, cols), bf),
+            pltpu.VMEM((peers, tok, cols), bf),
+            pltpu.VMEM((tok, feat), f32),
+            pltpu.VMEM((tok, LANES), f32),
+            pltpu.VMEM((tok, LANES), f32),
+            pltpu.VMEM((tok, LANES), f32),
+            pltpu.VMEM((LANES, tok), f32),
+            pltpu.VMEM((wide, tok), bf),
+            pltpu.VMEM((tok // 2, LANES), bf),
+            pltpu.VMEM((peers, tok // 2, LANES), bf),
+            pltpu.VMEM((tok // 2, LANES), bf),
+            pltpu.VMEM((peers, tok // 2, LANES), bf),
+            pltpu.VMEM((depth, wide, cols), bf),
+            pltpu.VMEM((depth, wide, cols), bf),
+            pltpu.VMEM((depth, 8, wide), f32),
+            dma((5,)),
+            dma((depth,)), dma((depth,)), dma((depth,)), dma((depth,)),
+            dma((2, depth)), dma((depth,)), dma((depth,)), dma((depth,)),
+            dma((2, depth)), dma((depth,)), dma((depth,)), dma((depth,)),
+            dma((peers,)), dma((peers,)), dma((peers,)), dma((peers,)),
+            dma((peers,)), dma((peers,)),
+            dma((depth,)), dma((depth,)), dma((depth,)),
+            dma((peers,)), dma((peers,)), dma((depth,)), dma((depth,)),
+        ],
+        compiler_params=pltpu.CompilerParams(
+            collective_id=0, has_side_effects=True, vmem_limit_bytes=60 * 1024 * 1024
+        ),
+    )(acts, a, weight, b, dy, slot_col, slot_row, cnt)
+    own = total[0].reshape(per, rank)[:, 0]
+    grad_down = sum_down.reshape(per, rank, feat).transpose(0, 2, 1)
+    grad_down = grad_down * (1.0 / own)[:, None, None]
+    grad_up = sum_up.reshape(per, rank, cols) * (adapter_scale / own)[:, None, None]
+    return (layer_out, ig, grad_down, grad_up)
+
+
+def local(mesh_sizes, groups, *args):
+    acts, weight, down, up, dy, _, adapter_slot = args
+    depth, pipes, peers = mesh_sizes
+    per, feat, rank = down.shape
+    tok, cols = dy.shape
+    fits = (
+        groups == 2 and depth == peers and LANES == 2 * rank and per * rank % LANES == 0
+        and cols % LANES == 0 and weight.shape[1] == cols and tok % 512 == 0
+        and feat % 1024 == 0 and per * rank <= 256 and cols <= 256 and tok * feat <= 1 << 21
+        and depth <= 4
+    )
+    if fits:
+        return fused(mesh_sizes, *args)
+    return plain(*args)
+
+
 def solution(mesh):
+    shape = mesh.shape
+    sizes = (shape["dp"], shape["pipe"], shape["tensor"] * shape["pipe"])
     return jax.shard_map(
-        local,
+        functools.partial(local, sizes, shape["groups"]),
         mesh=mesh,
         in_specs=(
             P(("groups", "dp"), TP),

time: 386 us -> 185 us (0.48)
  waiting for transfers between devices: 292 us -> 0 us
  Pallas kernels: 0 us -> 170 us
  matrix products: 46.1 us -> 0 us
  blocking collectives: 21.8 us -> 0 us
  between operations: 14.2 us -> 0.65 us
  local copies, waits for them, and re-layouts: 2.83 us -> 8.45 us
    pallas_call x0 -> x1, Pallas kernels: none -> 170 us  [fused(): pl.pallas_call(functools.partial(fused_kernel, (depth, pipes, peers, per,...]
    all_gather x3 -> x0, waiting for transfers between devices: 148 us -> none  [the longest x1 81.1 us: local(): weight_all = lax.all_gather(weight, 'dp', axis=1, tiled=True)]
    reduce_scatter x3 -> x0, waiting for transfers between devices: 113 us -> none  [the longest x1 77.4 us: local(): lax.psum_scatter(part_down, 'dp', scatter_dimension=0, tiled=True)]
    dot_general x8 -> x0, matrix products: 46.1 us -> none  [dot(): lax.dot_general(a, b, (dims, ((), ())), preferred_element_type=jnp.float32)]
    psum x1 -> x0, waiting for transfers between devices: 28.6 us -> none  [local(): low = spread(lax.psum(low, TP))]
    all_gather x1 -> x0, blocking collectives: 14.7 us -> none  [local(): lax.all_gather(up.reshape(per * rank, cols), 'dp', axis=0, tiled=True)]
    psum x1 -> x0, blocking collectives: 7.1 us -> none  [local(): counts = lax.psum(jnp.sum(slot_hot.astype(jnp.float32), axis=0), 'dp')]
  transfers between devices with their start and end apart: 7 -> 0, of which waited for: 6 -> 0; matrix products, arithmetic and copies ran while one was open for 11% -> 0% of each run, Pallas kernels for 0% -> 0%
where the time goes in v2:
time: 185 us
  Pallas kernels  170 us (92%)
  local copies, waits for them, and re-layouts  8.45 us (5%)
  other arithmetic  6.1 us (3%)
    pallas_call x1, Pallas kernels, fused(): pl.pallas_call(functools.partial(fused_kernel, (depth, pipes, peers, per,...  170 us

profile of v2, /device:TPU:3, one launch (start us, length us, event | category | flops | bytes accessed | tf_op | source)
XLA Modules:
  0.0 184.9 jit_solution(11778773506582761607)
XLA Ops:
  0.6 0.8 select_reduce_fusion
  1.4 0.1 convert_reduce_fusion
  1.5 0.1 broadcast_in_dim.46
  1.6 0.1 broadcast_in_dim.47
  1.7 0.1 broadcast_in_dim.48
  1.8 0.6 broadcast_in_dim.49.cnt_ref
  2.4 0.6 broadcast_in_dim.45.slot_row
  3.0 1.0 broadcast_in_dim.44.slot_col
  4.0 2.3 %copy.15.a_hbm = bf16[2048,256]{1,0:T(8,128)(2,1)} copy(bf16[2048,256]{0,1:T(8,128)(2,1)} %bitcast.15) | data formatting | bytes 2097152 | tf_op jit(solution)/shard_map/reshape | solution.py:534
  6.3 169.7 %shard_map.102 = (bf16[1024,256]{1,0:T(8,128)(2,1)}, bf16[1024,2048]{1,0:T(8,128)(2,1)}, f32[256,2048]{1,0:T(8,128)}, f32[256,256]{1,0:T(8,128)}, f32[8,256]{1,0:T(8,128)}) custom-call(bf16[1024,2048]{1,0:T(8,128)(2,1)} %x_hbm.1, bf16[2048,256]{1,0:T(8,128)(2,1)} %copy.15.a_hbm, bf16[2048,256]{1,0:T(8,128)(2,1)} %w_hbm.1, bf16[256,256]{1,0:T(8,128)(2,1)} %bitcast.17, ...), custom_call_target="tpu_custom_call" | custom-call | tf_op jit(solution)/shard_map/pallas_call | solution.py:540
  175.9 0.7 slice_reduce_fusion
  176.7 0.1 reshape_squeeze.3
  176.7 0.1 copy.17
  176.9 0.0 copy-start.1
  176.9 1.8 broadcast_multiply_fusion
  178.7 0.0 copy-start
  178.7 3.4 %multiply_bitcast_fusion = f32[4,2048,64]{1,2,0:T(8,128)} fusion(f32[4,64,2048]{2,1,0:T(8,128)} %bitcast.14, f32[4]{0:T(128)S(1)} %get-tuple-element.15), kind=kLoop, calls=%fused_computation | loop fusion | flops 524288 | bytes 4194320 | tf_op jit(solution)/shard_map/mul | solution.py:590
  182.0 0.0 copy-done.1
  182.0 0.8 copy.20
  182.8 0.0 copy-done
  182.8 2.0 %copy.21 = bf16[1024,2048]{1,0:T(8,128)(2,1)} copy(bf16[1024,2048]{1,0:T(8,128)(2,1)S(1)} %copy-done) | data formatting | bytes 8388608
  (1 shorter events, 0.0 us)
Async XLA Ops:
  176.9 5.2 %copy-start.1 = (bf16[1024,256]{1,0:T(8,128)(2,1)S(1)}, bf16[1024,256]{1,0:T(8,128)(2,1)}, u32[]{:S(2)}) copy-start(bf16[1024,256]{1,0:T(8,128)(2,1)} %get-tuple-element.20) | copy-start | bytes 1572868
  178.7 4.2 %copy-start = (bf16[1024,2048]{1,0:T(8,128)(2,1)S(1)}, bf16[1024,2048]{1,0:T(8,128)(2,1)}, u32[]{:S(2)}) copy-start(bf16[1024,2048]{1,0:T(8,128)(2,1)} %get-tuple-element.21) | copy-start | bytes 12582916

commit v3 on v2

--- a/solution.py
+++ b/solution.py
@@ -306,53 +306,57 @@
 
         tiles(tok // ROWS, body)
 
-    def make_part(d):
+    def make_part(d, h):
         transposed(grad_t, d)
 
         def body(c):
-            cols = rows_at(c, wide_cols)
+            cols = rows_at(c + h * half_tiles, wide_cols)
             part[d, :, cols] = dot(lhs[...], x[:, cols], ((1,), (0,))).astype(jnp.bfloat16)
 
-        tiles(feat // wide_cols, body)
-
-    def add_to_part(d, recv):
+        tiles(half_tiles, body)
+
+    half_tiles = half // wide_cols
+
+    def add_to_part(d, h, recv):
         def body(c):
-            cols = rows_at(c, wide_cols)
+            cols = rows_at(c + h * half_tiles, wide_cols)
             total = part[d, :, cols].astype(jnp.float32) + recv[d, :, cols].astype(jnp.float32)
             part[d, :, cols] = total.astype(jnp.bfloat16)
 
-        tiles(feat // wide_cols, body)
-
-    def rs_up(d, to):
-        return rc(part.at[d], recv_r.at[d], rs_ss.at[d], rr_rs.at[d], {"dp": to})
-
-    def rs_down(d, to):
-        return rc(part.at[d], recv_l.at[d], rs_ss.at[d], rl_rs.at[d], {"dp": to})
-
-    def reduce_step(t):
+        tiles(half_tiles, body)
+
+    def rs_up(d, h, to):
+        at = (d, slice(None), pl.ds(h * half, half))
+        return rc(part.at[at], recv_r.at[at], rs_ss.at[h, d], rr_rs.at[h, d], {"dp": to})
+
+    def rs_down(d, h, to):
+        at = (d, slice(None), pl.ds(h * half, half))
+        return rc(part.at[at], recv_l.at[at], rs_ss.at[h, d], rl_rs.at[h, d], {"dp": to})
+
+    def reduce_step(t, h):
         @pl.when(t >= i)
         def _():
             d = depth - 1 - t + i
-            make_part(d)
+            make_part(d, h)
 
             @pl.when(i > 0)
             def _():
-                rs_up(d, i + 1).wait_recv()
-                add_to_part(d, recv_r)
-
-            rs_up(d, i + 1).start()
+                rs_up(d, h, i + 1).wait_recv()
+                add_to_part(d, h, recv_r)
+
+            rs_up(d, h, i + 1).start()
 
         @pl.when(t >= depth - 1 - i)
         def _():
             d = i - (depth - 1 - t)
-            make_part(d)
+            make_part(d, h)
 
             @pl.when(i < depth - 1)
             def _():
-                rs_down(d, i - 1).wait_recv()
-                add_to_part(d, recv_l)
-
-            rs_down(d, i - 1).start()
+                rs_down(d, h, i - 1).wait_recv()
+                add_to_part(d, h, recv_l)
+
+            rs_down(d, h, i - 1).start()
 
     loads[0].wait()
     for q in range(1, depth):
@@ -400,22 +404,38 @@
         low_add(src)
         back_a(src, False)
 
-    for t in range(depth - 1):
-        reduce_step(t)
-        forward(a_all, az_ss, az_rs, ay_ss, ay_rs, t + 1)
-        if t == 0:
+    def forward_a(step):
+        forward(a_all, az_ss, az_rs, ay_ss, ay_rs, step)
+
+    def forward_w(step):
+        forward(w_all, wz_ss, wz_rs, wy_ss, wy_rs, step)
+
+    last = depth - 1
+    reduce_step(0, 0)
+    forward_a(1)
+    reduce_step(0, 1)
+    back_a(i, True)
+    for t in range(1, last):
+        forward_a(t + 1)
+        if t == 1:
             own_sends(w_all, wz_ss, wz_rs)
-            back_a(i, True)
-        else:
-            ways(t, use_a)
-    forward(w_all, wz_ss, wz_rs, wy_ss, wy_rs, 1)
-    ways(depth - 1, use_a)
+        ways(t, use_a)
+        reduce_step(t, 0)
+        if t > 1:
+            forward_w(t - 1)
+        reduce_step(t, 1)
+    if last == 1:
+        own_sends(w_all, wz_ss, wz_rs)
+    ways(last, use_a)
     pack(lpack_send)
     for q in range(1, peers):
         tp_copy(lpack_send, lpack_recv, l_ss, l_rs, (k + q) % peers, k).start()
     for q in range(1, peers):
         kk = (k + q) % peers
         dy_copy(kk, kk).wait_recv()
+    sent = max(0, last - 2)
+    if sent < last:
+        forward_w(sent + 1)
     back_w(i)
     unpack(lpack_send, lpack_recv, l_ss, l_rs, low, 1.0)
     grad_t[...] = jnp.transpose(low[...])
@@ -441,22 +461,25 @@
         base_block(src)
         back_w(src)
 
-    for s in range(2, depth):
-        forward(w_all, wz_ss, wz_rs, wy_ss, wy_rs, s)
-        ways(s - 1, use_w)
+    for step in range(sent + 2, depth):
+        forward_w(step)
+        ways(step - 1, use_w)
+    for step in range(1, min(sent + 1, last)):
+        ways(step, use_w)
 
     grad_t[...] = jnp.transpose(grad_low[...])
-    make_part(i)
-
-    @pl.when(i > 0)
-    def _():
-        rs_up(i, (i + 1) % depth).wait_recv()
-        add_to_part(i, recv_r)
-
-    @pl.when(i < depth - 1)
-    def _():
-        rs_down(i, (i + 1) % depth).wait_recv()
-        add_to_part(i, recv_l)
+    for h in range(2):
+        make_part(i, h)
+
+        @pl.when(i > 0)
+        def _():
+            rs_up(i, h, (i + 1) % depth).wait_recv()
+            add_to_part(i, h, recv_r)
+
+        @pl.when(i < depth - 1)
+        def _():
+            rs_down(i, h, (i + 1) % depth).wait_recv()
+            add_to_part(i, h, recv_l)
 
     def down_out(c):
         cols = rows_at(c, wide_cols)
@@ -508,7 +531,8 @@
         b_copy(j, i).wait_send()
         c_copy(j, i).wait_send()
         up_copy(j, i).wait_send()
-        rs_up(j, j).wait_send()
+        rs_up(j, 0, j).wait_send()
+        rs_up(j, 1, j).wait_send()
     for q in range(1, peers):
         kk = (k + q) % peers
         tp_copy(gpack_send, gpack_recv, g_ss, g_rs, kk, k).wait_send()
@@ -578,7 +602,7 @@
             dma((2, depth)), dma((depth,)), dma((depth,)), dma((depth,)),
             dma((peers,)), dma((peers,)), dma((peers,)), dma((peers,)),
             dma((peers,)), dma((peers,)),
-            dma((depth,)), dma((depth,)), dma((depth,)),
+            dma((2, depth)), dma((2, depth)), dma((2, depth)),
             dma((peers,)), dma((peers,)), dma((depth,)), dma((depth,)),
         ],
         compiler_params=pltpu.CompilerParams(

time: 185 us -> 178 us (0.962)
  Pallas kernels: 170 us -> 163 us
    pallas_call x1, Pallas kernels: 170 us -> 163 us  [fused(): pl.pallas_call(functools.partial(fused_kernel, (depth, pipes, peers, per,...]
where the time goes in v3:
time: 178 us
  Pallas kernels  163 us (92%)
  local copies, waits for them, and re-layouts  8.45 us (5%)
  other arithmetic  6.1 us (3%)
    pallas_call x1, Pallas kernels, fused(): pl.pallas_call(functools.partial(fused_kernel, (depth, pipes, peers, per,...  163 us

profile of v3, /device:TPU:3, one launch (start us, length us, event | category | flops | bytes accessed | tf_op | source)
XLA Modules:
  0.0 178.1 jit_solution(9854183146016699545)
XLA Ops:
  0.6 0.8 select_reduce_fusion
  1.4 0.1 convert_reduce_fusion
  1.5 0.1 broadcast_in_dim.46
  1.6 0.1 broadcast_in_dim.47
  1.7 0.1 broadcast_in_dim.48
  1.8 0.6 broadcast_in_dim.49.cnt_ref
  2.4 0.6 broadcast_in_dim.45.slot_row
  3.0 1.0 broadcast_in_dim.44.slot_col
  4.0 2.3 %copy.15.a_hbm = bf16[2048,256]{1,0:T(8,128)(2,1)} copy(bf16[2048,256]{0,1:T(8,128)(2,1)} %bitcast.15) | data formatting | bytes 2097152 | tf_op jit(solution)/shard_map/reshape | solution.py:558
  6.3 162.9 %shard_map.102 = (bf16[1024,256]{1,0:T(8,128)(2,1)}, bf16[1024,2048]{1,0:T(8,128)(2,1)}, f32[256,2048]{1,0:T(8,128)}, f32[256,256]{1,0:T(8,128)}, f32[8,256]{1,0:T(8,128)}) custom-call(bf16[1024,2048]{1,0:T(8,128)(2,1)} %x_hbm.1, bf16[2048,256]{1,0:T(8,128)(2,1)} %copy.15.a_hbm, bf16[2048,256]{1,0:T(8,128)(2,1)} %w_hbm.1, bf16[256,256]{1,0:T(8,128)(2,1)} %bitcast.17, ...), custom_call_target="tpu_custom_call" | custom-call | tf_op jit(solution)/shard_map/pallas_call | solution.py:564
  169.1 0.7 slice_reduce_fusion
  169.9 0.1 reshape_squeeze.3
  169.9 0.1 copy.17
  170.1 0.0 copy-start.1
  170.1 1.8 %broadcast_multiply_fusion = f32[4,64,256]{2,1,0:T(8,128)} fusion(f32[4,64,256]{2,1,0:T(8,128)} %bitcast.16, f32[4]{0:T(128)S(1)} %get-tuple-element.14), kind=kLoop, calls=%fused_computation.1 | loop fusion | flops 65536 | bytes 524304 | tf_op jit(solution)/shard_map/mul | solution.py:615
  171.9 0.0 copy-start
  171.9 3.4 %multiply_bitcast_fusion = f32[4,2048,64]{1,2,0:T(8,128)} fusion(f32[4,64,2048]{2,1,0:T(8,128)} %bitcast.14, f32[4]{0:T(128)S(1)} %get-tuple-element.15), kind=kLoop, calls=%fused_computation | loop fusion | flops 524288 | bytes 4194320 | tf_op jit(solution)/shard_map/mul | solution.py:614
  175.2 0.0 copy-done.1
  175.2 0.8 copy.20
  176.0 0.0 copy-done
  176.0 2.0 %copy.21 = bf16[1024,2048]{1,0:T(8,128)(2,1)} copy(bf16[1024,2048]{1,0:T(8,128)(2,1)S(1)} %copy-done) | data formatting | bytes 8388608
  (1 shorter events, 0.0 us)
Async XLA Ops:
  170.1 5.2 %copy-start.1 = (bf16[1024,256]{1,0:T(8,128)(2,1)S(1)}, bf16[1024,256]{1,0:T(8,128)(2,1)}, u32[]{:S(2)}) copy-start(bf16[1024,256]{1,0:T(8,128)(2,1)} %get-tuple-element.20) | copy-start | bytes 1572868
  171.9 4.2 %copy-start = (bf16[1024,2048]{1,0:T(8,128)(2,1)S(1)}, bf16[1024,2048]{1,0:T(8,128)(2,1)}, u32[]{:S(2)}) copy-start(bf16[1024,2048]{1,0:T(8,128)(2,1)} %get-tuple-element.21) | copy-start | bytes 12582916

commit v4 on v3

--- a/solution.py
+++ b/solution.py
@@ -394,6 +394,7 @@
         tp_copy(gpack_send, gpack_recv, g_ss, g_rs, (k + q) % peers, k).start()
     for q in range(1, peers):
         dy_copy((k + q) % peers, k).start()
+    own_sends(w_all, wz_ss, wz_rs)
     fold[...] = jnp.zeros_like(fold)
     low_add(i)
     unpack(gpack_send, gpack_recv, g_ss, g_rs, grad_low, adapter_scale)
@@ -416,16 +417,15 @@
     reduce_step(0, 1)
     back_a(i, True)
     for t in range(1, last):
-        forward_a(t + 1)
         if t == 1:
-            own_sends(w_all, wz_ss, wz_rs)
+            forward_a(2)
+        forward_w(t)
         ways(t, use_a)
         reduce_step(t, 0)
-        if t > 1:
-            forward_w(t - 1)
+        if t + 2 <= last:
+            forward_a(t + 2)
         reduce_step(t, 1)
-    if last == 1:
-        own_sends(w_all, wz_ss, wz_rs)
+    forward_w(last)
     ways(last, use_a)
     pack(lpack_send)
     for q in range(1, peers):
@@ -433,9 +433,6 @@
     for q in range(1, peers):
         kk = (k + q) % peers
         dy_copy(kk, kk).wait_recv()
-    sent = max(0, last - 2)
-    if sent < last:
-        forward_w(sent + 1)
     back_w(i)
     unpack(lpack_send, lpack_recv, l_ss, l_rs, low, 1.0)
     grad_t[...] = jnp.transpose(low[...])
@@ -461,10 +458,7 @@
         base_block(src)
         back_w(src)
 
-    for step in range(sent + 2, depth):
-        forward_w(step)
-        ways(step - 1, use_w)
-    for step in range(1, min(sent + 1, last)):
+    for step in range(1, last):
         ways(step, use_w)
 
     grad_t[...] = jnp.transpose(grad_low[...])

time: 178 us -> 153 us (0.86)
  Pallas kernels: 163 us -> 138 us
    pallas_call x1, Pallas kernels: 163 us -> 138 us  [fused(): pl.pallas_call(functools.partial(fused_kernel, (depth, pipes, peers, per,...]
where the time goes in v4:
time: 153 us
  Pallas kernels  138 us (90%)
  local copies, waits for them, and re-layouts  8.45 us (6%)
  other arithmetic  6.1 us (4%)
    pallas_call x1, Pallas kernels, fused(): pl.pallas_call(functools.partial(fused_kernel, (depth, pipes, peers, per,...  138 us
    mul x1, other arithmetic, fused(): grad_down = grad_down * (1.0 / own)[:, None, None]  3.39 us

profile of v4, /device:TPU:3, one launch (start us, length us, event | category | flops | bytes accessed | tf_op | source)
XLA Modules:
  0.0 153.1 jit_solution(16942066899654746638)
XLA Ops:
  0.6 0.8 select_reduce_fusion
  1.4 0.1 convert_reduce_fusion
  1.5 0.1 broadcast_in_dim.46
  1.6 0.1 broadcast_in_dim.47
  1.7 0.1 broadcast_in_dim.48
  1.8 0.6 broadcast_in_dim.49.cnt_ref
  2.4 0.6 broadcast_in_dim.45.slot_row
  3.0 1.0 broadcast_in_dim.44.slot_col
  4.0 2.3 %copy.15.a_hbm = bf16[2048,256]{1,0:T(8,128)(2,1)} copy(bf16[2048,256]{0,1:T(8,128)(2,1)} %bitcast.15) | data formatting | bytes 2097152 | tf_op jit(solution)/shard_map/reshape | solution.py:552
  6.3 137.9 %shard_map.102 = (bf16[1024,256]{1,0:T(8,128)(2,1)}, bf16[1024,2048]{1,0:T(8,128)(2,1)}, f32[256,2048]{1,0:T(8,128)}, f32[256,256]{1,0:T(8,128)}, f32[8,256]{1,0:T(8,128)}) custom-call(bf16[1024,2048]{1,0:T(8,128)(2,1)} %x_hbm.1, bf16[2048,256]{1,0:T(8,128)(2,1)} %copy.15.a_hbm, bf16[2048,256]{1,0:T(8,128)(2,1)} %w_hbm.1, bf16[256,256]{1,0:T(8,128)(2,1)} %bitcast.17, ...), custom_call_target="tpu_custom_call" | custom-call | tf_op jit(solution)/shard_map/pallas_call | solution.py:558
  144.1 0.7 slice_reduce_fusion
  144.9 0.1 reshape_squeeze.3
  144.9 0.1 copy.17
  145.1 0.0 copy-start.1
  145.1 1.8 %broadcast_multiply_fusion = f32[4,64,256]{2,1,0:T(8,128)} fusion(f32[4,64,256]{2,1,0:T(8,128)} %bitcast.16, f32[4]{0:T(128)S(1)} %get-tuple-element.14), kind=kLoop, calls=%fused_computation.1 | loop fusion | flops 65536 | bytes 524304 | tf_op jit(solution)/shard_map/mul | solution.py:609
  146.9 0.0 copy-start
  146.9 3.4 %multiply_bitcast_fusion = f32[4,2048,64]{1,2,0:T(8,128)} fusion(f32[4,64,2048]{2,1,0:T(8,128)} %bitcast.14, f32[4]{0:T(128)S(1)} %get-tuple-element.15), kind=kLoop, calls=%fused_computation | loop fusion | flops 524288 | bytes 4194320 | tf_op jit(solution)/shard_map/mul | solution.py:608
  150.2 0.0 copy-done.1
  150.2 0.8 copy.20
  151.0 0.0 copy-done
  151.0 2.0 %copy.21 = bf16[1024,2048]{1,0:T(8,128)(2,1)} copy(bf16[1024,2048]{1,0:T(8,128)(2,1)S(1)} %copy-done) | data formatting | bytes 8388608
  (1 shorter events, 0.0 us)
Async XLA Ops:
  145.1 5.2 %copy-start.1 = (bf16[1024,256]{1,0:T(8,128)(2,1)S(1)}, bf16[1024,256]{1,0:T(8,128)(2,1)}, u32[]{:S(2)}) copy-start(bf16[1024,256]{1,0:T(8,128)(2,1)} %get-tuple-element.20) | copy-start | bytes 1572868
  146.9 4.2 %copy-start = (bf16[1024,2048]{1,0:T(8,128)(2,1)S(1)}, bf16[1024,2048]{1,0:T(8,128)(2,1)}, u32[]{:S(2)}) copy-start(bf16[1024,2048]{1,0:T(8,128)(2,1)} %get-tuple-element.21) | copy-start | bytes 12582916
